TPU v7x, 32 devices: a whole 2x2x4 slice. The times are simulated.
32 devices in a mesh: lat: 4 (over y, x), lon: 8 (over z, core).
Axes of the slice: x: 2, y: 2, z: 4, core: 2. Of those that a mesh axis runs over, the one named last changes fastest.
Arguments:
- tokens: bfloat16 [32, 256, 1024], P('lat', 'lon'), may hold values from -40 to 40
- ln_gain: float32 [1024], replicated, may hold values from 0.1 to 1.9
- w_qkv: bfloat16 [1024, 1536], replicated, may hold values from -0.34375 to 0.34375
- bias_table: float32 [8, 225], replicated, may hold values from -4 to 4
- bias_index: int32 [64, 64], replicated, may hold values from 0 to 224
- cap_group: int32 [2, 64, 4, 1], P(None, 'lon'), may hold values from 0 to 7; in each aligned block of 32 rows (0 to 31, 32 to 63, ..., all dimensions but the last counted through in order) at most 8 rows name the same one
Outputs:
- mixed: bfloat16 [32, 256, 512], P('lat', 'lon')
Inputs may be any that keep to these rules, and one draw needn't show every extreme that they name: `cap_group`: within one pole, the 32 tiles of one longitude sector name any one group at most 8 times, and some sector names some group exactly 8 times.
All inputs are finite; a program needn't handle non-finite values.
Results may differ from a plain program's by a relative error of at most 0.0079.
Values may be sent and summed in bfloat16 or wider, within the bound.
A program may use at most 128 MiB of HBM per device.

v0:
```python
import jax
import jax.numpy as jnp
from jax import lax
from jax.sharding import PartitionSpec as P

D = 1024
HEADS = 8
HD = 64
WIN = 8
TW = 4
CAP = 4
RH = 8
RW = 32
HW = 512
HALF = 4
BIAS_ROWS = 225
TILES_DEV = 32


epsilon = 1e-05
masked_score = -1e30


def with_halo(block, sides, width, periodic):
    for axis, dim in sides:
        count = lax.axis_size(axis)
        forward = [(i, i + 1) for i in range(count - 1)]
        if periodic:
            forward.append((count - 1, 0))
        backward = [(target, source) for source, target in forward]
        low = lax.ppermute(
            lax.slice_in_dim(block, block.shape[dim] - width, None, axis=dim), axis, forward
        )
        high = lax.ppermute(lax.slice_in_dim(block, 0, width, axis=dim), axis, backward)
        block = jnp.concatenate([low, block, high], axis=dim)
    return block


def layer_norm(row_tokens, ln_gain):
    values = row_tokens.astype(jnp.float32)
    center = jnp.mean(values, axis=-1, keepdims=True)
    spread = jnp.mean(jnp.square(values - center), axis=-1, keepdims=True)
    return ((values - center) * lax.rsqrt(spread + epsilon) * ln_gain).astype(jnp.bfloat16)


def softmax_bf16(scores):
    highest = jnp.max(scores, axis=-1, keepdims=True)
    raised = jnp.exp(scores - highest)
    return (raised / jnp.sum(raised, axis=-1, keepdims=True)).astype(jnp.bfloat16)


def local(tokens, ln_gain, w_qkv, bias_table, bias_index, cap_group):
    lat_index = lax.axis_index("lat")
    lat_count = lax.axis_size("lat")
    lon_count = lax.axis_size("lon")
    att_scale = HD ** (-0.5)
    normed = layer_norm(tokens, ln_gain)
    projected = jnp.dot(
        normed.reshape(RH * RW, D), w_qkv, preferred_element_type=jnp.float32
    ).astype(jnp.bfloat16)
    grid_proj = projected.reshape(RH, RW, 3 * HW)
    queries = grid_proj[:, :, :HW]
    keys_values = grid_proj[:, :, HW:]
    wider = with_halo(keys_values, (("lon", 1),), HALF, True)
    extended = with_halo(wider, (("lat", 0),), HALF, False)
    is_north = lat_index == 0
    is_polar = is_north | (lat_index == lat_count - 1)
    cap_start = jnp.where(is_north, 0, RH - CAP).astype(jnp.int32)
    tile_cols = RW // TW
    group_ids = jnp.where(is_north, cap_group[0], cap_group[1]).reshape(TILES_DEV)
    most_slots = 2 * TILES_DEV // lon_count
    slot_total = lon_count * most_slots
    group_hot = (group_ids[:, None] == jnp.arange(lon_count, dtype=jnp.int32)[None, :]).astype(
        jnp.int32
    )
    earlier = jnp.cumsum(group_hot, axis=0) - group_hot
    slot_rank = jnp.sum(earlier * group_hot, axis=1)
    slot_of = group_ids * most_slots + slot_rank
    dispatch = (jnp.arange(slot_total, dtype=jnp.int32)[:, None] == slot_of[None, :]).astype(
        jnp.bfloat16
    )
    slot_valid = jnp.sum(dispatch, axis=1).reshape(lon_count, most_slots)
    channels = grid_proj.shape[-1]
    cap_rows = lax.dynamic_slice_in_dim(grid_proj, cap_start, CAP, 0)
    cap_rows = cap_rows.reshape(CAP, tile_cols, TW, channels).transpose(1, 0, 2, 3)
    packed = jnp.dot(
        dispatch, cap_rows.reshape(TILES_DEV, TW * channels), preferred_element_type=jnp.float32
    ).astype(jnp.bfloat16)
    arrived, arrived_valid = (
        lax.all_to_all(
            packed.reshape(lon_count, most_slots, TW, 3 * HW),
            "lon",
            split_axis=0,
            concat_axis=0,
            tiled=True,
        ),
        lax.all_to_all(slot_valid, "lon", split_axis=0, concat_axis=0, tiled=True),
    )
    slot_proj = arrived.reshape(-1, 3 * HW)
    token_valid = jnp.broadcast_to(arrived_valid.reshape(-1, 1), (slot_total, TW)).reshape(-1) > 0.5
    cap_q = slot_proj[:, :HW].reshape(-1, HEADS, HD)
    cap_k = slot_proj[:, HW : 2 * HW].reshape(-1, HEADS, HD)
    cap_v = slot_proj[:, 2 * HW :].reshape(-1, HEADS, HD)
    cap_scores = (
        jnp.einsum("qhd,khd->hqk", cap_q, cap_k, preferred_element_type=jnp.float32) * att_scale
    )
    cap_scores = jnp.where(token_valid[None, None, :], cap_scores, masked_score)
    cap_weights = softmax_bf16(cap_scores)
    cap_result = jnp.einsum(
        "hqk,khd->qhd", cap_weights, cap_v, preferred_element_type=jnp.float32
    ).astype(jnp.bfloat16)
    returned = lax.all_to_all(
        cap_result.reshape(lon_count, most_slots, TW, HW),
        "lon",
        split_axis=0,
        concat_axis=0,
        tiled=True,
    )
    position_hot = (
        bias_index[:, :, None] == jnp.arange(BIAS_ROWS, dtype=jnp.int32)[None, None, :]
    ).astype(jnp.float32)
    position_bias = jnp.einsum(
        "pqt,ht->hpq", position_hot, bias_table, precision=lax.Precision.HIGHEST
    )
    ext_rows = RH + WIN
    ext_cols = RW + WIN
    win_rows = ext_rows // WIN
    win_cols = ext_cols // WIN
    padded_q = jnp.pad(queries, ((HALF, HALF), (HALF, HALF), (0, 0)))
    grid_q = padded_q.reshape(win_rows, WIN, win_cols, WIN, HEADS, HD)
    grid_k = extended[:, :, :HW].reshape(win_rows, WIN, win_cols, WIN, HEADS, HD)
    grid_v = extended[:, :, HW:].reshape(win_rows, WIN, win_cols, WIN, HEADS, HD)
    global_row = lat_index * RH - HALF + jnp.arange(ext_rows, dtype=jnp.int32)
    row_valid = (global_row >= 0) & (global_row < RH * lat_count)
    key_valid = jnp.broadcast_to(row_valid.reshape(win_rows, WIN, 1), (win_rows, WIN, WIN)).reshape(
        win_rows, 1, 1, 1, WIN * WIN
    )
    scores = jnp.einsum(
        "aibjhd,akblhd->abhijkl", grid_q, grid_k, preferred_element_type=jnp.float32
    )
    scores = (
        scores.reshape(win_rows, win_cols, HEADS, WIN * WIN, WIN * WIN) * att_scale
        + position_bias[None, None]
    )
    scores = jnp.where(key_valid, scores, masked_score)
    weights = softmax_bf16(scores).reshape(win_rows, win_cols, HEADS, WIN, WIN, WIN, WIN)
    win_out = jnp.einsum(
        "abhijkl,akblhd->aibjhd", weights, grid_v, preferred_element_type=jnp.float32
    )
    win_grid = win_out.reshape(ext_rows, ext_cols, HW)[HALF : HALF + RH, HALF : HALF + RW]
    tile_out = jnp.dot(
        dispatch.T, returned.reshape(slot_total, TW * HW), preferred_element_type=jnp.float32
    )
    cap_rows = tile_out.reshape(tile_cols, CAP, TW, HW).transpose(1, 0, 2, 3).reshape(CAP, RW, HW)
    cap_rows = jnp.where(is_polar, cap_rows, 0.0)
    cap_grid = lax.dynamic_update_slice_in_dim(
        jnp.zeros((RH, RW, HW), jnp.float32), cap_rows, cap_start, 0
    )
    return (win_grid + cap_grid).astype(jnp.bfloat16)


def solution(mesh):
    placed = (P("lat", "lon", None), P(), P(), P(), P(), P(None, "lon", None, None))
    return jax.shard_map(
        local, mesh=mesh, in_specs=placed, out_specs=P("lat", "lon", None), check_vma=False
    )
```

profile of v0, /device:TPU:1, one launch (start us, length us, event | category | flops | bytes accessed | tf_op | source)
XLA Modules:
  0.0 136.7 jit_solution(9101166519928422374)
XLA Ops:
  2.1 6.4 %all-to-all-start.1 = ((bf16[8,1,8]{2,1,0:T(2,128)(2,1)}), bf16[8,1,8]{2,1,0:T(2,128)(2,1)S(1)}, u32[]{:S(2)}, u32[]{:S(2)}) async-start(bf16[8,1,8]{2,1,0:T(2,128)(2,1)} %all_to_all.16), calls=%async_computation.1 | async-start | bytes 8192 | tf_op jit(solution)/shard_map/all_to_all | solution.py:97
  20.1 4.2 %fusion.16 = f32[8,64,64]{2,0,1:T(8,128)} fusion(s32[64,64]{1,0:T(8,128)} %param.10, f32[8,225]{1,0:T(8,128)} %param.9), kind=kOutput, calls=%fused_computation.30 | convolution fusion | flops 89395200 | bytes 154656 | tf_op jit(solution)/shard_map/pqt,ht->hpq/dot_general | solution.py:122
  26.5 3.9 %collective-permute-start.2 = (bf16[4,40,1024]{2,1,0:T(8,128)(2,1)}, bf16[4,40,1024]{2,1,0:T(8,128)(2,1)}, u32[]{:S(2)}, u32[]{:S(2)}) collective-permute-start(bf16[4,40,1024]{2,1,0:T(8,128)(2,1)} %get-tuple-element.12), channel_id=1, source_target_pairs={{0,8},{8,16},{16,24},{1,9},{9,17},{17,25},{2,10},{10,18},{18,26},{... | collective-permute-start | bytes 983048 | tf_op jit(solution)/shard_map/ppermute | solution.py:31
  32.6 2.6 %reshape.183 = bf16[2,8,5,8,8,64]{5,4,3,2,1,0:T(8,128)(2,1)} reshape(bf16[16,40,512]{2,1,0:T(8,128)(2,1)} %pad.4) | data formatting | bytes 1310720 | tf_op jit(solution)/shard_map/reshape | solution.py:130
  35.2 2.8 %add.58 = f32[8,8,8,8,8]{4,3,0,2,1:T(8,128)} reshape(f32[8,64,64]{2,0,1:T(8,128)} %fusion.16) | data formatting | bytes 262144 | tf_op jit(solution)/shard_map/add | solution.py:142
  38.1 3.2 %copy.89 = f32[8,8,8,8,8]{2,4,3,1,0:T(8,128)} copy(f32[8,8,8,8,8]{4,3,0,2,1:T(8,128)} %add.58) | data formatting | bytes 262144 | tf_op jit(solution)/shard_map/add | solution.py:142
  41.3 6.3 %all-to-all-start = ((bf16[8,8,4,1536]{3,2,1,0:T(4,128)(2,1)}), bf16[8,8,4,1536]{3,2,1,0:T(4,128)(2,1)}, u32[]{:S(2)}, u32[]{:S(2)}) async-start(bf16[8,8,4,1536]{3,2,1,0:T(4,128)(2,1)} %copy.96), calls=%async_computation | async-start | bytes 1572864 | tf_op jit(solution)/shard_map/all_to_all | solution.py:90
  50.6 2.6 %reshape.182 = bf16[2,8,5,8,8,64]{5,4,3,2,1,0:T(8,128)(2,1)} reshape(bf16[16,40,512]{2,1,0:T(8,128)(2,1)} %get-tuple-element.5) | data formatting | bytes 1310720 | tf_op jit(solution)/shard_map/reshape | solution.py:132
  53.2 2.6 %reshape.184 = bf16[2,8,5,8,8,64]{5,4,3,2,1,0:T(8,128)(2,1)} reshape(bf16[16,40,512]{2,1,0:T(8,128)(2,1)} %get-tuple-element.6) | data formatting | bytes 1310720 | tf_op jit(solution)/shard_map/reshape | solution.py:131
  55.9 20.6 %fusion.2 = (f32[2,5,8,8,8]{4,3,2,1,0:T(8,128)S(1)}, f32[2,5,8,8,8,8,8]{4,6,5,3,2,1,0:T(8,128)}) fusion(f32[8,8,8,8,8]{2,4,3,1,0:T(8,128)} %copy.89, pred[2,8]{1,0:T(4,128)(4,1)S(1)} %compare_and_fusion, bf16[2,8,5,8,8,64,1]{5,4,3,2,1,0,6:T(8,128)(2,1)} %bitcast.64, bf16[2,8,5,8,8,64,1]{5,4,3,2,1,0,6:T(8,128)(2,1)} %bitcast.63), kind=kOutput, calls=%fused_computation.5 | convolution fusion | flops 43248640 | bytes 2773008 | tf_op jit(solution)/shard_map/aibjhd,akblhd->abhijkl/dot_general | solution.py:138
  76.5 11.8 %fusion.1 = f32[2,5,8,8,8]{4,3,2,1,0:T(8,128)} fusion(f32[2,5,8,8,8,8,8]{4,6,5,3,2,1,0:T(8,128)} %get-tuple-element.15, f32[2,5,8,8,8]{4,3,2,1,0:T(8,128)S(1)} %get-tuple-element.14, f32[8,8,8,8,8]{2,4,3,1,0:T(8,128)S(1)} %copy-done.1, pred[2,8]{1,0:T(4,128)(4,1)S(1)} %compare_and_fusion), kind=kLoop, calls=%fused_computation.4 | loop fusion | flops 1633280 | bytes 1482768 | tf_op jit(solution)/shard_map/reduce_sum | solution.py:49
  88.3 2.3 %reshape.189 = bf16[256,1536]{1,0:T(8,128)(2,1)} reshape(bf16[8,8,4,1536]{3,2,1,0:T(4,128)(2,1)} %all-to-all-done) | data formatting | bytes 1572864 | tf_op jit(solution)/shard_map/reshape | solution.py:99
  90.6 2.0 %fusion.38 = (bf16[256,512]{1,0:T(8,128)(2,1)}, bf16[256,512]{1,0:T(8,128)(2,1)}, bf16[256,512]{1,0:T(8,128)(2,1)}) fusion(bf16[256,1536]{1,0:T(8,128)(2,1)} %reshape.189), kind=kLoop, calls=%fused_computation.65 | loop fusion | bytes 1572864 | tf_op jit(solution)/shard_map/slice | solution.py:102
  92.6 1.8 %copy.100 = bf16[256,512]{0,1:T(8,128)(2,1)} copy(bf16[256,512]{1,0:T(8,128)(2,1)} %get-tuple-element.7) | data formatting | bytes 524288 | tf_op jit(solution)/shard_map/slice | solution.py:102
  94.4 1.8 %copy.99 = bf16[256,512]{0,1:T(8,128)(2,1)} copy(bf16[256,512]{1,0:T(8,128)(2,1)} %get-tuple-element.8) | data formatting | bytes 524288 | tf_op jit(solution)/shard_map/slice | solution.py:101
  98.0 3.2 %fusion.41 = (f32[8,256]{1,0:T(8,128)S(1)}, f32[8,256,256]{1,2,0:T(8,128)}) fusion(pred[256]{0:T(512)(128)(4,1)S(1)} %gt.20, bf16[256,8,64]{0,2,1:T(8,128)(2,1)} %bitcast.77, bf16[256,8,64]{0,2,1:T(8,128)(2,1)} %bitcast.76), kind=kOutput, calls=%fused_computation.68 | convolution fusion | flops 69206272 | bytes 2629888 | tf_op jit(solution)/shard_map/sub | solution.py:48
  101.2 2.7 %fusion.15 = bf16[256,8,64]{0,2,1:T(8,128)(2,1)} fusion(bf16[256,8,64]{0,2,1:T(8,128)(2,1)} %bitcast.78, f32[8,256,256]{1,2,0:T(8,128)} %get-tuple-element.17, f32[8,256]{1,0:T(8,128)S(1)} %get-tuple-element.16), kind=kOutput, calls=%fused_computation.29 | convolution fusion | flops 68288512 | bytes 2629632 | tf_op jit(solution)/shard_map/hqk,khd->qhd/dot_general | solution.py:109
  103.9 2.0 %copy.102 = bf16[256,8,64]{2,1,0:T(8,128)(2,1)} copy(bf16[256,8,64]{0,2,1:T(8,128)(2,1)} %fusion.15) | data formatting | bytes 524288 | tf_op jit(solution)/shard_map/convert_element_type | solution.py:111
  106.0 2.1 %reshape.193 = bf16[8,8,4,512]{3,2,1,0:T(4,128)(2,1)} reshape(bf16[256,8,64]{2,1,0:T(8,128)(2,1)} %copy.102) | data formatting | bytes 524288 | tf_op jit(solution)/shard_map/reshape | solution.py:113
  108.0 5.1 %all-to-all-start.2 = ((bf16[8,8,4,512]{3,2,1,0:T(4,128)(2,1)}), bf16[8,8,4,512]{3,2,1,0:T(4,128)(2,1)}, u32[]{:S(2)}, u32[]{:S(2)}) async-start(bf16[8,8,4,512]{3,2,1,0:T(4,128)(2,1)} %reshape.193), calls=%async_computation.2 | async-start | bytes 524288 | tf_op jit(solution)/shard_map/all_to_all | solution.py:112
  113.2 10.8 %fusion.7 = f32[2,8,5,8,8,64]{5,3,1,4,2,0:T(8,128)S(1)} fusion(f32[2,5,8,8,8,8,8]{4,6,5,3,2,1,0:T(8,128)} %get-tuple-element.15, f32[2,5,8,8,8]{4,3,2,1,0:T(8,128)} %fusion.1, f32[2,5,8,8,8]{4,3,2,1,0:T(8,128)S(1)} %get-tuple-element.14, f32[8,8,8,8,8]{2,4,3,1,0:T(8,128)} %copy.89, pred[2,8]{1,0:T(4,128)(4,1)S(1)} %compare_and_fusion, ...), kind=kOutput, calls=%fused_computation.16 | convolution fusion | flops 43909120 | bytes 3448848 | tf_op jit(solution)/shard_map/abhijkl,akblhd->aibjhd/dot_general | solution.py:147
  124.0 3.0 %copy.92 = f32[2,8,5,8,8,64]{5,4,3,2,1,0:T(8,128)} copy(f32[2,8,5,8,8,64]{5,3,1,4,2,0:T(8,128)S(1)} %fusion.7) | data formatting | bytes 2621440 | tf_op jit(solution)/shard_map/abhijkl,akblhd->aibjhd/transpose | solution.py:147
  127.0 2.9 %reshape.185 = f32[16,40,512]{2,1,0:T(8,128)} reshape(f32[2,8,5,8,8,64]{5,4,3,2,1,0:T(8,128)} %copy.92) | data formatting | bytes 2621440 | tf_op jit(solution)/shard_map/reshape | solution.py:150
  129.9 1.9 %slice.69 = f32[8,32,512]{2,1,0:T(8,128)} slice(f32[16,40,512]{2,1,0:T(8,128)} %reshape.185), slice={[4:12], [4:36], [0:512]} | slice | bytes 1048576 | tf_op jit(solution)/shard_map/slice | solution.py:150
  (56 shorter events, 27.7 us)
Async XLA Ops:
  0.0 12.4 %copy-start = (bf16[1024,1536]{1,0:T(8,128)(2,1)S(1)}, bf16[1024,1536]{1,0:T(8,128)(2,1)}, u32[]{:S(2)}) copy-start(bf16[1024,1536]{1,0:T(8,128)(2,1)} %param.8) | copy-start | bytes 9437188
  2.1 39.2 %all-to-all-start.1 = ((bf16[8,1,8]{2,1,0:T(2,128)(2,1)}), bf16[8,1,8]{2,1,0:T(2,128)(2,1)S(1)}, u32[]{:S(2)}, u32[]{:S(2)}) async-start(bf16[8,1,8]{2,1,0:T(2,128)(2,1)} %all_to_all.16), calls=%async_computation.1 | async-start | bytes 8192 | tf_op jit(solution)/shard_map/all_to_all | solution.py:97
  13.4 2.5 %copy-start.2 = (bf16[256,1536]{1,0:T(8,128)(2,1)}, bf16[256,1536]{1,0:T(8,128)(2,1)S(1)}, u32[]{:S(2)}) copy-start(bf16[256,1536]{1,0:T(8,128)(2,1)S(1)} %convolution_convert_fusion.1) | copy-start | bytes 2359300
  14.2 10.1 %collective-permute-start = (bf16[8,4,1024]{2,1,0:T(4,128)(2,1)}, bf16[8,4,1024]{2,1,0:T(4,128)(2,1)S(1)}, u32[]{:S(2)}, u32[]{:S(2)}) collective-permute-start(bf16[8,4,1024]{2,1,0:T(4,128)(2,1)} %get-tuple-element.10), channel_id=1, source_target_pairs={{0,1},{1,2},{2,3},{3,4},{4,5},{5,6},{6,7},{7,0},{8,9},{9,10},{10,1... | collective-permute-start | bytes 196616 | tf_op jit(solution)/shard_map/ppermute | solution.py:31
  15.8 8.5 %collective-permute-start.1 = (bf16[8,4,1024]{2,1,0:T(4,128)(2,1)}, bf16[8,4,1024]{2,1,0:T(4,128)(2,1)S(1)}, u32[]{:S(2)}, u32[]{:S(2)}) collective-permute-start(bf16[8,4,1024]{2,1,0:T(4,128)(2,1)} %get-tuple-element.11), channel_id=1, source_target_pairs={{1,0},{2,1},{3,2},{4,3},{5,4},{6,5},{7,6},{0,7},{9,8},{10,9},{11,1... | collective-permute-start | bytes 196616 | tf_op jit(solution)/shard_map/ppermute | solution.py:34
  26.5 21.5 %collective-permute-start.2 = (bf16[4,40,1024]{2,1,0:T(8,128)(2,1)}, bf16[4,40,1024]{2,1,0:T(8,128)(2,1)}, u32[]{:S(2)}, u32[]{:S(2)}) collective-permute-start(bf16[4,40,1024]{2,1,0:T(8,128)(2,1)} %get-tuple-element.12), channel_id=1, source_target_pairs={{0,8},{8,16},{16,24},{1,9},{9,17},{17,25},{2,10},{10,18},{18,26},{... | collective-permute-start | bytes 983048 | tf_op jit(solution)/shard_map/ppermute | solution.py:31
  30.4 17.6 %collective-permute-start.3 = (bf16[4,40,1024]{2,1,0:T(8,128)(2,1)}, bf16[4,40,1024]{2,1,0:T(8,128)(2,1)}, u32[]{:S(2)}, u32[]{:S(2)}) collective-permute-start(bf16[4,40,1024]{2,1,0:T(8,128)(2,1)} %get-tuple-element.13), channel_id=1, source_target_pairs={{8,0},{16,8},{24,16},{9,1},{17,9},{25,17},{10,2},{18,10},{26,18},{... | collective-permute-start | bytes 983048 | tf_op jit(solution)/shard_map/ppermute | solution.py:34
  41.3 47.0 %all-to-all-start = ((bf16[8,8,4,1536]{3,2,1,0:T(4,128)(2,1)}), bf16[8,8,4,1536]{3,2,1,0:T(4,128)(2,1)}, u32[]{:S(2)}, u32[]{:S(2)}) async-start(bf16[8,8,4,1536]{3,2,1,0:T(4,128)(2,1)} %copy.96), calls=%async_computation | async-start | bytes 1572864 | tf_op jit(solution)/shard_map/all_to_all | solution.py:90
  55.9 20.6 %copy-start.1 = (f32[8,8,8,8,8]{2,4,3,1,0:T(8,128)S(1)}, f32[8,8,8,8,8]{2,4,3,1,0:T(8,128)}, u32[]{:S(2)}) copy-start(f32[8,8,8,8,8]{2,4,3,1,0:T(8,128)} %copy.89) | copy-start | bytes 393220
  108.0 23.8 %all-to-all-start.2 = ((bf16[8,8,4,512]{3,2,1,0:T(4,128)(2,1)}), bf16[8,8,4,512]{3,2,1,0:T(4,128)(2,1)}, u32[]{:S(2)}, u32[]{:S(2)}) async-start(bf16[8,8,4,512]{3,2,1,0:T(4,128)(2,1)} %reshape.193), calls=%async_computation.2 | async-start | bytes 524288 | tf_op jit(solution)/shard_map/all_to_all | solution.py:112
where the time goes:
time: 139 us; the launch traced here: 137 us
  local copies, waits for them, and re-layouts  44.4 us (32%)
  matrix products  44.1 us (32%)
  starting transfers between devices  24.6 us (18%)
  other arithmetic  23.3 us (17%)
    dot_general x1, matrix products, local(): jnp.einsum('aibjhd,akblhd->abhijkl', grid_q, grid_k, preferred_element_ty...  20.6 us
    reduce_sum x1, other arithmetic, softmax_bf16(): jnp.sum(raised, axis=-1, keepdims=True)  11.8 us
    dot_general x1, matrix products, local(): jnp.einsum('abhijkl,akblhd->aibjhd', weights, grid_v, preferred_element_t...  10.8 us
    all_to_all x1, starting transfers between devices, local(): lax.all_to_all(slot_valid, 'lon', split_axis=0, concat_axis=0, tiled=True)  6.38 us
    all_to_all x1, starting transfers between devices, local(): lax.all_to_all(packed.reshape(lon_count, most_slots, TW, 3 * HW), 'lon',...  6.32 us
    add x2, local copies, waits for them, and re-layouts, local(): scores.reshape(win_rows, win_cols, HEADS, WIN * WIN, WIN * WIN) * att_scale  6.07 us
    ppermute x2, starting transfers between devices, with_halo(): lax.ppermute(lax.slice_in_dim(block, block.shape[dim] - width, None, axis...  5.5 us
    all_to_all x1, starting transfers between devices, local(): lax.all_to_all(cap_result.reshape(lon_count, most_slots, TW, HW), 'lon',...  5.13 us
  transfers between devices with their start and end apart: 7, of which 0 were waited for; matrix products, arithmetic and copies ran while one was open for 62% of the time, Pallas kernels for 0%

commit v1 on v0

v1 whole, which is shorter than its diff:
```python
import functools

import jax
import jax.numpy as jnp
from jax import lax
from jax.experimental import pallas as pl
from jax.experimental.pallas import tpu as pltpu
from jax.sharding import PartitionSpec as P

MESH = pl.DeviceIdType.MESH
HEADS = 8
HD = 64
HW = 512
STRIP = 128
QUAD = 16
EXT = STRIP + 2 * QUAD
PAIRS = HEADS // 2
epsilon = 1e-05
masked_score = -1e30
f32, bf16 = jnp.float32, jnp.bfloat16


def one_hot(rows, columns, source):
    row = lax.broadcasted_iota(jnp.int32, (rows, columns), 0)
    column = lax.broadcasted_iota(jnp.int32, (rows, columns), 1)
    return jnp.where(source(row) == column, 1.0, 0.0).astype(bf16)


def grid_token(n):
    strip, block, row, column = n // STRIP, (n // QUAD) % 8, (n // 4) % 4, n % 4
    return (strip * 4 + row) * 32 + block * 4 + column


def block_token(n):
    row, column = n // 32, n % 32
    return (row // 4) * STRIP + (column // 4) * QUAD + (row % 4) * 4 + column % 4


def window_position(n):
    high, side, row, column = n // 32, (n // QUAD) % 2, (n // 4) % 4, n % 4
    return (high * 4 + row) * 8 + side * 4 + column


def dot(a, b):
    return jnp.dot(a, b, preferred_element_type=f32)


def dot_t(a, b):
    return lax.dot_general(a, b, (((1,), (1,)), ((), ())), preferred_element_type=f32)


def layer_norm(x, gain):
    values = x.astype(f32)
    center = jnp.mean(values, axis=-1, keepdims=True)
    values = values - center
    spread = jnp.mean(values * values, axis=-1, keepdims=True)
    return (values * lax.rsqrt(spread + epsilon) * gain).astype(bf16)


def softmax_bf16(scores):
    raised = jnp.exp(scores - jnp.max(scores, axis=-1, keepdims=True))
    return (raised * (1.0 / jnp.sum(raised, axis=-1, keepdims=True))).astype(bf16)


def swap_halves(x):
    return jnp.concatenate([x[:, HD:], x[:, :HD]], axis=1)


def kernel(
    lat_n, lon_n, x_hbm, gain_ref, w_hbm, table_ref, index_ref, group_ref, out_ref,
    x_ref, w_ref, own, halo, q_ref, kv_ref, bias_ref, cap_send, cap_recv, ret_send, ret_recv, acc,
    load_sem, hs_sem, hr_sem, cs_sem, cr_sem, rs_sem, rr_sem,
):
    lat, lon = lax.axis_index("lat"), lax.axis_index("lon")
    west, east = lax.rem(lon + lon_n - 1, lon_n), lax.rem(lon + 1, lon_n)
    has_n, has_s = lat > 0, lat < lat_n - 1
    polar = (lat == 0) | (lat == lat_n - 1)
    x_copy = pltpu.make_async_copy(x_hbm, x_ref, load_sem.at[0])
    w_copy = pltpu.make_async_copy(w_hbm, w_ref, load_sem.at[1])
    x_copy.start()
    w_copy.start()

    barrier = pltpu.get_barrier_semaphore()

    def greet(a, o):
        pl.semaphore_signal(barrier, inc=1, device_id=(a, o), device_id_type=MESH)

    greet(lat, west)
    greet(lat, east)

    @pl.when(has_n)
    def _():
        for o in (west, lon, east):
            greet(lat - 1, o)

    @pl.when(has_s)
    def _():
        for o in (west, lon, east):
            greet(lat + 1, o)

    @pl.when(polar)
    def _():
        @pl.loop(2, lon_n - 1)
        def _(o):
            greet(lat, lax.rem(lon + o, lon_n))

    x_copy.wait()
    own[...] = dot(one_hot(2 * STRIP, 2 * STRIP, grid_token), x_ref[...]).astype(bf16)

    as_int = lambda flag: jnp.where(flag, 1, 0)
    pl.semaphore_wait(
        barrier, 2 + 3 * as_int(has_n) + 3 * as_int(has_s) + (lon_n - 3) * as_int(polar)
    )

    def halo_copy(slot, source, target, rows, a, o):
        return pltpu.make_async_remote_copy(
            src_ref=own.at[pl.ds(source, rows)],
            dst_ref=halo.at[pl.ds(target, rows)],
            send_sem=hs_sem.at[slot],
            recv_sem=hr_sem.at[slot],
            device_id=(a, o),
            device_id_type=MESH,
        )

    last = STRIP - QUAD
    north = [
        halo_copy(0, 0, EXT + QUAD, STRIP, lat - 1, lon),
        halo_copy(1, 0, EXT + EXT - QUAD, QUAD, lat - 1, west),
        halo_copy(2, last, EXT, QUAD, lat - 1, east),
    ]
    south = [
        halo_copy(3, STRIP, QUAD, STRIP, lat + 1, lon),
        halo_copy(4, STRIP, EXT - QUAD, QUAD, lat + 1, west),
        halo_copy(5, STRIP + last, 0, QUAD, lat + 1, east),
    ]
    sides = [
        halo_copy(6, 0, 2 * EXT + 2 * QUAD, QUAD, lat, west),
        halo_copy(7, STRIP, 2 * EXT + 3 * QUAD, QUAD, lat, west),
        halo_copy(8, last, 2 * EXT, QUAD, lat, east),
        halo_copy(9, STRIP + last, 2 * EXT + QUAD, QUAD, lat, east),
    ]

    @pl.when(has_n)
    def _():
        for c in north:
            c.start()

    @pl.when(has_s)
    def _():
        for c in south:
            c.start()

    for c in sides:
        c.start()

    gain = gain_ref[...]
    normed = layer_norm(own[...], gain)
    w_copy.wait()
    q_ref[...] = (dot(normed, w_ref[:, :HW]).astype(bf16) * HD ** (-0.5)).astype(bf16)
    for part in range(2):
        got = dot(normed, w_ref[:, (part + 1) * HW : (part + 2) * HW]).astype(bf16)
        kv_ref[1, QUAD : QUAD + STRIP, part * HW : (part + 1) * HW] = got[:STRIP]
        kv_ref[2, QUAD : QUAD + STRIP, part * HW : (part + 1) * HW] = got[STRIP:]

    head0 = lax.rem(lon, HEADS)
    base = lon - head0

    def cap_copy(o):
        d = lax.rem(lon + o, lon_n)
        return pltpu.make_async_remote_copy(
            src_ref=cap_send.at[lax.rem(d, HEADS)],
            dst_ref=cap_recv.at[lon],
            send_sem=cs_sem.at[o],
            recv_sem=cr_sem.at[o],
            device_id=(lat, d),
            device_id_type=MESH,
        )

    def ret_copy(j):
        d = base + lax.rem(head0 + j, HEADS)
        return pltpu.make_async_remote_copy(
            src_ref=ret_send.at[j],
            dst_ref=ret_recv.at[head0],
            send_sem=rs_sem.at[j],
            recv_sem=rr_sem.at[j],
            device_id=(lat, d),
            device_id_type=MESH,
        )

    def cap_pack(strip):
        lane = lax.broadcasted_iota(jnp.int32, (4, STRIP), 1)
        row = lax.broadcasted_iota(jnp.int32, (4, STRIP), 0)
        spread = jnp.where((lane // 4) % 4 == row, 1.0, 0.0).astype(bf16)
        ids = dot(group_ref[strip].astype(f32).astype(bf16), spread)
        block = lax.broadcasted_iota(jnp.int32, (8, STRIP), 0)
        where = lax.broadcasted_iota(jnp.int32, (8, STRIP), 1) // QUAD
        ids = jnp.sum(jnp.where(block == where, ids, 0.0), axis=0, keepdims=True)
        ids = jnp.broadcast_to(ids, (QUAD, STRIP)).astype(bf16)
        for h in range(HEADS):
            k = kv_ref[1 + strip, QUAD : QUAD + STRIP, h * HD : (h + 1) * HD]
            v = kv_ref[1 + strip, QUAD : QUAD + STRIP, HW + h * HD : HW + (h + 1) * HD]
            q = q_ref[strip * STRIP : (strip + 1) * STRIP, h * HD : (h + 1) * HD]
            cap_send[h, :STRIP] = jnp.concatenate([k, v], axis=1)
            cap_send[h, STRIP : STRIP + HD] = jnp.concatenate([q[:HD], q[HD:]], axis=1)
            cap_send[h, STRIP + HD :] = ids

    @pl.when(lat == 0)
    def _():
        cap_pack(0)

    @pl.when(lat == lat_n - 1)
    def _():
        cap_pack(1)

    @pl.when(polar)
    def _():
        @pl.loop(1, lon_n)
        def _(o):
            cap_copy(o).start()

        cap_recv[lon] = cap_send[head0]

    order = one_hot(64, 64, window_position)
    index = index_ref[...].astype(f32).astype(bf16)
    index = dot_t(dot(order, index).astype(bf16), order).astype(jnp.int32)
    index = jnp.concatenate([index, index], axis=1)
    table = table_ref[...]
    table_low = table[:, :128]
    table_high = jnp.concatenate(
        [table[:, 128:], jnp.zeros((HEADS, 256 - table.shape[1]), f32)], axis=1
    )
    key = lax.broadcasted_iota(jnp.int32, (64, 64), 1)
    for h in range(HEADS):
        low = jnp.take_along_axis(
            jnp.broadcast_to(table_low[h : h + 1], (64, 128)), index & 127, axis=1,
            mode="promise_in_bounds",
        )
        high = jnp.take_along_axis(
            jnp.broadcast_to(table_high[h : h + 1], (64, 128)), index & 127, axis=1,
            mode="promise_in_bounds",
        )
        bias = jnp.where(index < 128, low, high)[:, :64]
        at = (h % 2) * 32
        north_bias = jnp.where((key < 32) & (lat == 0), masked_score, bias)
        south_bias = jnp.where((key >= 32) & (lat == lat_n - 1), masked_score, bias)
        bias_ref[0, h // 2, at : at + 32] = north_bias[32:]
        bias_ref[1, h // 2, at : at + 32] = south_bias[:32]

    @pl.when(has_n)
    def _():
        for c in south:
            c.wait_recv()

    @pl.when(has_s)
    def _():
        for c in north:
            c.wait_recv()

    for c in sides:
        c.wait_recv()

    @pl.when(jnp.logical_not(has_n))
    def _():
        halo[:EXT] = jnp.zeros((EXT, halo.shape[1]), bf16)

    @pl.when(jnp.logical_not(has_s))
    def _():
        halo[EXT : 2 * EXT] = jnp.zeros((EXT, halo.shape[1]), bf16)

    normed = layer_norm(halo[...], gain)
    for part in range(2):
        columns = slice(part * HW, (part + 1) * HW)
        got = dot(normed, w_ref[:, (part + 1) * HW : (part + 2) * HW]).astype(bf16)
        kv_ref[0, :, columns] = got[:EXT]
        kv_ref[3, :, columns] = got[EXT : 2 * EXT]
        for s in range(2):
            at = 2 * EXT + s * QUAD
            kv_ref[1 + s, :QUAD, columns] = got[at : at + QUAD]
            kv_ref[1 + s, EXT - QUAD :, columns] = got[at + 2 * QUAD : at + 3 * QUAD]

    left = lax.broadcasted_iota(jnp.int32, (1, 128), 1) < HD

    @pl.when(polar)
    def _():
        @pl.loop(1, lon_n)
        def _(o):
            cap_copy(o).wait_recv()

        kv = jnp.concatenate([cap_recv[t, :STRIP] for t in range(lon_n)], axis=0)
        key_group = jnp.concatenate(
            [cap_recv[t, STRIP + HD :].astype(f32)[:1] for t in range(lon_n)], axis=1
        )
        diagonal = lax.broadcasted_iota(jnp.int32, (STRIP, STRIP), 0) == lax.broadcasted_iota(
            jnp.int32, (STRIP, STRIP), 1
        )

        def block(s):
            packed = cap_recv[s, STRIP : STRIP + HD].astype(f32)
            q = jnp.concatenate([packed, swap_halves(packed)], axis=0)
            q = jnp.where(left, q, 0.0).astype(bf16)
            ids = cap_recv[s, STRIP + HD :].astype(f32)[:1]
            group = jnp.sum(jnp.where(diagonal, ids, 0.0), axis=1, keepdims=True)
            scores = jnp.where(group == key_group, dot_t(q, kv), masked_score)
            result = dot(softmax_bf16(scores), kv)
            return jnp.where(left, swap_halves(result[:HD]), result[HD:]).astype(bf16)

        @pl.loop(1, HEADS)
        def _(j):
            ret_send[j] = block(base + lax.rem(head0 + j, HEADS))
            ret_copy(j).start()

        ret_recv[head0] = block(lon)

    keep = [jnp.where(left, 1.0, 0.0).astype(bf16), jnp.where(left, 0.0, 1.0).astype(bf16)]
    for a in range(2):
        for w in range(5):
            if w == 0:
                first, count, skip = 0, QUAD, QUAD
            elif w == 4:
                first, count, skip = STRIP - QUAD, QUAD, 0
            else:
                first, count, skip = QUAD + 32 * (w - 1), 32, 0
            first += a * STRIP
            for pair in range(PAIRS):
                lanes = slice(pair * 128, (pair + 1) * 128)
                v_lanes = slice(HW + pair * 128, HW + (pair + 1) * 128)
                rows = slice(32 * w, 32 * w + 32)
                k = jnp.concatenate([kv_ref[2 * a, rows, lanes], kv_ref[2 * a + 1, rows, lanes]], axis=0)
                v = jnp.concatenate(
                    [kv_ref[2 * a, rows, v_lanes], kv_ref[2 * a + 1, rows, v_lanes]], axis=0
                )
                q = q_ref[first : first + count, lanes]
                q = jnp.concatenate([q * keep[0], q * keep[1]], axis=0)
                bias = jnp.concatenate(
                    [
                        bias_ref[a, pair, skip : skip + count],
                        bias_ref[a, pair, 32 + skip : 32 + skip + count],
                    ],
                    axis=0,
                )
                result = dot(softmax_bf16(dot_t(q, k) + bias), v)
                acc[first : first + count, lanes] = jnp.where(left, result[:count], result[count:])

    def add_cap(strip):
        for pair in range(PAIRS):
            lanes = slice(pair * 128, (pair + 1) * 128)
            even, odd = ret_recv[2 * pair].astype(f32), ret_recv[2 * pair + 1].astype(f32)
            at = strip * STRIP
            acc[at : at + HD, lanes] += jnp.where(left, even, swap_halves(odd))
            acc[at + HD : at + STRIP, lanes] += jnp.where(left, swap_halves(even), odd)

    @pl.when(polar)
    def _():
        @pl.loop(1, HEADS)
        def _(j):
            ret_copy(j).wait_recv()

    @pl.when(lat == 0)
    def _():
        add_cap(0)

    @pl.when(lat == lat_n - 1)
    def _():
        add_cap(1)

    mixed = acc[...].astype(bf16)
    out_ref[...] = dot(one_hot(2 * STRIP, 2 * STRIP, block_token), mixed).astype(bf16)

    @pl.when(has_n)
    def _():
        for c in north:
            c.wait_send()

    @pl.when(has_s)
    def _():
        for c in south:
            c.wait_send()

    for c in sides:
        c.wait_send()

    @pl.when(polar)
    def _():
        @pl.loop(1, lon_n)
        def _(o):
            cap_copy(o).wait_send()

        @pl.loop(1, HEADS)
        def _(j):
            ret_copy(j).wait_send()


def local(tokens, ln_gain, w_qkv, bias_table, bias_index, cap_group):
    lat_n, lon_n = lax.axis_size("lat"), lax.axis_size("lon")
    rows, columns, width = tokens.shape
    count = rows * columns
    vmem = pl.BlockSpec(memory_space=pltpu.VMEM)
    anywhere = pl.BlockSpec(memory_space=pl.ANY)
    out = pl.pallas_call(
        functools.partial(kernel, lat_n, lon_n),
        out_shape=jax.ShapeDtypeStruct((count, HW), bf16),
        in_specs=[anywhere, vmem, anywhere, vmem, vmem, vmem],
        out_specs=vmem,
        scratch_shapes=[
            pltpu.VMEM((count, width), bf16),
            pltpu.VMEM(w_qkv.shape, bf16),
            pltpu.VMEM((count, width), bf16),
            pltpu.VMEM((2 * EXT + 4 * QUAD, width), bf16),
            pltpu.VMEM((count, HW), bf16),
            pltpu.VMEM((4, EXT, 2 * HW), bf16),
            pltpu.VMEM((2, PAIRS, 64, 64), f32),
            pltpu.VMEM((HEADS, STRIP + HD + QUAD, 128), bf16),
            pltpu.VMEM((lon_n, STRIP + HD + QUAD, 128), bf16),
            pltpu.VMEM((HEADS, HD, 128), bf16),
            pltpu.VMEM((HEADS, HD, 128), bf16),
            pltpu.VMEM((count, HW), f32),
            pltpu.SemaphoreType.DMA((2,)),
            pltpu.SemaphoreType.DMA((10,)),
            pltpu.SemaphoreType.DMA((10,)),
            pltpu.SemaphoreType.DMA((lon_n,)),
            pltpu.SemaphoreType.DMA((lon_n,)),
            pltpu.SemaphoreType.DMA((HEADS,)),
            pltpu.SemaphoreType.DMA((HEADS,)),
        ],
        compiler_params=pltpu.CompilerParams(
            collective_id=0, has_side_effects=True, vmem_limit_bytes=48 * 1024 * 1024
        ),
    )(
        tokens.reshape(count, width), ln_gain.reshape(1, width), w_qkv, bias_table, bias_index,
        cap_group.reshape(cap_group.shape[:3]),
    )
    return out.reshape(rows, columns, HW)


def solution(mesh):
    placed = (P("lat", "lon", None), P(), P(), P(), P(), P(None, "lon", None, None))
    return jax.shard_map(
        local, mesh=mesh, in_specs=placed, out_specs=P("lat", "lon", None), check_vma=False
    )
```

time: 139 us -> 45.2 us (0.33)
  the two profiles are of different devices: /device:TPU:1 before, /device:TPU:7 now
where the time goes in v1:
time: 45.2 us; the launch traced here: 44.9 us
  Pallas kernels  38.3 us (85%)
  local copies, waits for them, and re-layouts  6.54 us (14%)
    pallas_call x1, Pallas kernels, local(): pl.pallas_call(functools.partial(kernel, lat_n, lon_n), out_shape=jax.Sha...  38.3 us
    unnamed x11, local copies, waits for them, and re-layouts  5.78 us

profile of v1, /device:TPU:7, one launch (start us, length us, event | category | flops | bytes accessed | tf_op | source)
XLA Modules:
  0.0 44.9 jit_solution(1393833313641229092)
XLA Ops:
  0.0 0.8 %copy.7.group_ref = s32[2,8,4]{2,1,0:T(8,128)S(1)} copy(s32[2,8,4]{1,2,0:T(4,128)} %bitcast.7) | data formatting | bytes 512 | tf_op jit(solution)/shard_map/reshape | solution.py:430
  0.8 0.0 copy-start
  0.8 1.9 %copy-done = bf16[1024,1536]{1,0:T(8,128)(2,1)S(1)} copy-done((bf16[1024,1536]{1,0:T(8,128)(2,1)S(1)}, bf16[1024,1536]{1,0:T(8,128)(2,1)}, u32[]{:S(2)}) %copy-start) | copy-done | bytes 3145752
  2.7 0.0 copy-start.1
  2.7 1.0 %copy-done.1 = bf16[8,32,1024]{2,1,0:T(8,128)(2,1)S(1)} copy-done((bf16[8,32,1024]{2,1,0:T(8,128)(2,1)S(1)}, bf16[8,32,1024]{2,1,0:T(8,128)(2,1)}, u32[]{:S(2)}) %copy-start.1) | copy-done | bytes 524312
  3.7 0.0 copy-start.2
  3.7 0.8 %copy-done.2 = s32[64,64]{1,0:T(8,128)S(1)} copy-done((s32[64,64]{1,0:T(8,128)S(1)}, s32[64,64]{1,0:T(8,128)}, u32[]{:S(2)}) %copy-start.2) | copy-done | bytes 16408
  4.5 0.0 copy-start.3
  4.5 0.7 %copy-done.3 = f32[8,225]{1,0:T(8,128)S(1)} copy-done((f32[8,225]{1,0:T(8,128)S(1)}, f32[8,225]{1,0:T(8,128)}, u32[]{:S(2)}) %copy-start.3) | copy-done | bytes 7224
  5.2 0.0 copy-start.4
  5.2 0.7 %copy-done.4 = f32[1024]{0:T(1024)S(1)} copy-done((f32[1024]{0:T(1024)S(1)}, f32[1024]{0:T(1024)}, u32[]{:S(2)}) %copy-start.4) | copy-done | bytes 4120
  5.8 38.3 %shard_map.64 = bf16[256,512]{1,0:T(8,128)(2,1)S(1)} custom-call(bf16[256,1024]{1,0:T(8,128)(2,1)S(1)} %bitcast.5, f32[1,1024]{1,0:T(1,128)S(1)} %bitcast.6, bf16[1024,1536]{1,0:T(8,128)(2,1)S(1)} %copy-done, f32[8,225]{1,0:T(8,128)S(1)} %copy-done.3, s32[64,64]{1,0:T(8,128)S(1)} %copy-done.2, s32[2,8,4]{2,1,0:T(8,128)S(1)} %copy.7.group_ref), custom_call_target="tpu_custom_call" | custom-call | tf_op jit(solution)/shard_map/pallas_call | solution.py:399
  44.2 0.7 %copy.9 = bf16[8,32,512]{2,1,0:T(8,128)(2,1)} copy(bf16[8,32,512]{2,1,0:T(8,128)(2,1)S(1)} %bitcast.4) | data formatting | bytes 524288
Async XLA Ops:
  0.8 1.9 %copy-start = (bf16[1024,1536]{1,0:T(8,128)(2,1)S(1)}, bf16[1024,1536]{1,0:T(8,128)(2,1)}, u32[]{:S(2)}) copy-start(bf16[1024,1536]{1,0:T(8,128)(2,1)} %w_hbm.1) | copy-start | bytes 9437188
  2.7 1.0 %copy-start.1 = (bf16[8,32,1024]{2,1,0:T(8,128)(2,1)S(1)}, bf16[8,32,1024]{2,1,0:T(8,128)(2,1)}, u32[]{:S(2)}) copy-start(bf16[8,32,1024]{2,1,0:T(8,128)(2,1)} %param.6) | copy-start | bytes 1572868
  3.7 0.8 %copy-start.2 = (s32[64,64]{1,0:T(8,128)S(1)}, s32[64,64]{1,0:T(8,128)}, u32[]{:S(2)}) copy-start(s32[64,64]{1,0:T(8,128)} %index_ref.1) | copy-start | bytes 49156
  4.5 0.7 %copy-start.3 = (f32[8,225]{1,0:T(8,128)S(1)}, f32[8,225]{1,0:T(8,128)}, u32[]{:S(2)}) copy-start(f32[8,225]{1,0:T(8,128)} %table_ref.1) | copy-start | bytes 21604
  5.2 0.7 %copy-start.4 = (f32[1024]{0:T(1024)S(1)}, f32[1024]{0:T(1024)}, u32[]{:S(2)}) copy-start(f32[1024]{0:T(1024)} %param.7) | copy-start | bytes 12292

commit v2 on v1

--- a/solution.py
+++ b/solution.py
@@ -67,8 +67,8 @@
 
 
 def kernel(
-    lat_n, lon_n, x_hbm, gain_ref, w_hbm, table_ref, index_ref, group_ref, out_ref,
-    x_ref, w_ref, own, halo, q_ref, kv_ref, bias_ref, cap_send, cap_recv, ret_send, ret_recv, acc,
+    lat_n, lon_n, x_hbm, gain_hbm, w_hbm, table_hbm, index_hbm, group_hbm, out_ref,
+    x_ref, w_ref, gain_ref, table_ref, index_ref, group_ref, own, halo, q_ref, kv_ref, bias_ref, cap_send, cap_recv, ret_send, ret_recv, acc,
     load_sem, hs_sem, hr_sem, cs_sem, cr_sem, rs_sem, rr_sem,
 ):
     lat, lon = lax.axis_index("lat"), lax.axis_index("lon")
@@ -77,8 +77,12 @@
     polar = (lat == 0) | (lat == lat_n - 1)
     x_copy = pltpu.make_async_copy(x_hbm, x_ref, load_sem.at[0])
     w_copy = pltpu.make_async_copy(w_hbm, w_ref, load_sem.at[1])
-    x_copy.start()
-    w_copy.start()
+    gain_copy = pltpu.make_async_copy(gain_hbm, gain_ref, load_sem.at[2])
+    table_copy = pltpu.make_async_copy(table_hbm, table_ref, load_sem.at[3])
+    index_copy = pltpu.make_async_copy(index_hbm, index_ref, load_sem.at[4])
+    group_copy = pltpu.make_async_copy(group_hbm, group_ref, load_sem.at[5])
+    for c in (x_copy, gain_copy, w_copy, index_copy, table_copy, group_copy):
+        c.start()
 
     barrier = pltpu.get_barrier_semaphore()
 
@@ -153,14 +157,22 @@
     for c in sides:
         c.start()
 
+    gain_copy.wait()
     gain = gain_ref[...]
-    normed = layer_norm(own[...], gain)
-    w_copy.wait()
-    q_ref[...] = (dot(normed, w_ref[:, :HW]).astype(bf16) * HD ** (-0.5)).astype(bf16)
-    for part in range(2):
-        got = dot(normed, w_ref[:, (part + 1) * HW : (part + 2) * HW]).astype(bf16)
-        kv_ref[1, QUAD : QUAD + STRIP, part * HW : (part + 1) * HW] = got[:STRIP]
-        kv_ref[2, QUAD : QUAD + STRIP, part * HW : (part + 1) * HW] = got[STRIP:]
+    cap_strip = jnp.where(lat == lat_n - 1, 1, 0)
+
+    def project(strip, wait):
+        rows = pl.ds(pl.multiple_of(strip * STRIP, STRIP), STRIP)
+        normed = layer_norm(own[rows], gain)
+        if wait:
+            w_copy.wait()
+        q_ref[rows] = (dot(normed, w_ref[:, :HW]).astype(bf16) * HD ** (-0.5)).astype(bf16)
+        got = dot(normed, w_ref[:, HW:]).astype(bf16)
+        kv_ref[1 + strip, QUAD : QUAD + STRIP] = got
+
+    project(cap_strip, True)
+    for c in (index_copy, table_copy, group_copy):
+        c.wait()
 
     head0 = lax.rem(lon, HEADS)
     base = lon - head0
@@ -188,37 +200,35 @@
         )
 
     def cap_pack(strip):
-        lane = lax.broadcasted_iota(jnp.int32, (4, STRIP), 1)
-        row = lax.broadcasted_iota(jnp.int32, (4, STRIP), 0)
-        spread = jnp.where((lane // 4) % 4 == row, 1.0, 0.0).astype(bf16)
-        ids = dot(group_ref[strip].astype(f32).astype(bf16), spread)
+        rows = pl.ds(pl.multiple_of(strip * STRIP, STRIP), STRIP)
+        lane = lax.broadcasted_iota(jnp.int32, (8, STRIP), 1)
         block = lax.broadcasted_iota(jnp.int32, (8, STRIP), 0)
-        where = lax.broadcasted_iota(jnp.int32, (8, STRIP), 1) // QUAD
-        ids = jnp.sum(jnp.where(block == where, ids, 0.0), axis=0, keepdims=True)
+        spread = jnp.where(lane // QUAD == block, 1.0, 0.0).astype(bf16)
+        ids = jnp.zeros((1, STRIP), f32)
+        for t in range(4):
+            row = group_ref[strip, t].astype(f32).astype(bf16)
+            row = dot(jnp.broadcast_to(row, (8, 8)), spread)[:1]
+            ids = jnp.where((lane[:1] // 4) % 4 == t, row, ids)
         ids = jnp.broadcast_to(ids, (QUAD, STRIP)).astype(bf16)
         for h in range(HEADS):
             k = kv_ref[1 + strip, QUAD : QUAD + STRIP, h * HD : (h + 1) * HD]
             v = kv_ref[1 + strip, QUAD : QUAD + STRIP, HW + h * HD : HW + (h + 1) * HD]
-            q = q_ref[strip * STRIP : (strip + 1) * STRIP, h * HD : (h + 1) * HD]
+            q = q_ref[rows, h * HD : (h + 1) * HD]
             cap_send[h, :STRIP] = jnp.concatenate([k, v], axis=1)
             cap_send[h, STRIP : STRIP + HD] = jnp.concatenate([q[:HD], q[HD:]], axis=1)
             cap_send[h, STRIP + HD :] = ids
 
-    @pl.when(lat == 0)
-    def _():
-        cap_pack(0)
-
-    @pl.when(lat == lat_n - 1)
-    def _():
-        cap_pack(1)
-
     @pl.when(polar)
     def _():
+        cap_pack(cap_strip)
+
         @pl.loop(1, lon_n)
         def _(o):
             cap_copy(o).start()
 
         cap_recv[lon] = cap_send[head0]
+
+    project(1 - cap_strip, False)
 
     order = one_hot(64, 64, window_position)
     index = index_ref[...].astype(f32).astype(bf16)
@@ -246,6 +256,39 @@
         bias_ref[0, h // 2, at : at + 32] = north_bias[32:]
         bias_ref[1, h // 2, at : at + 32] = south_bias[:32]
 
+    left = lax.broadcasted_iota(jnp.int32, (1, 128), 1) < HD
+
+    @pl.when(polar)
+    def _():
+        @pl.loop(1, lon_n)
+        def _(o):
+            cap_copy(o).wait_recv()
+
+        kv = jnp.concatenate([cap_recv[t, :STRIP] for t in range(lon_n)], axis=0)
+        key_group = jnp.concatenate(
+            [cap_recv[t, STRIP + HD :].astype(f32)[:1] for t in range(lon_n)], axis=1
+        )
+        diagonal = lax.broadcasted_iota(jnp.int32, (STRIP, STRIP), 0) == lax.broadcasted_iota(
+            jnp.int32, (STRIP, STRIP), 1
+        )
+
+        def block(s):
+            packed = cap_recv[s, STRIP : STRIP + HD].astype(f32)
+            q = jnp.concatenate([packed, swap_halves(packed)], axis=0)
+            q = jnp.where(left, q, 0.0).astype(bf16)
+            ids = cap_recv[s, STRIP + HD :].astype(f32)[:1]
+            group = jnp.sum(jnp.where(diagonal, ids, 0.0), axis=1, keepdims=True)
+            scores = jnp.where(group == key_group, dot_t(q, kv), masked_score)
+            result = dot(softmax_bf16(scores), kv)
+            return jnp.where(left, swap_halves(result[:HD]), result[HD:]).astype(bf16)
+
+        @pl.loop(1, HEADS)
+        def _(j):
+            ret_send[j] = block(base + lax.rem(head0 + j, HEADS))
+            ret_copy(j).start()
+
+        ret_recv[head0] = block(lon)
+
     @pl.when(has_n)
     def _():
         for c in south:
@@ -278,41 +321,9 @@
             kv_ref[1 + s, :QUAD, columns] = got[at : at + QUAD]
             kv_ref[1 + s, EXT - QUAD :, columns] = got[at + 2 * QUAD : at + 3 * QUAD]
 
-    left = lax.broadcasted_iota(jnp.int32, (1, 128), 1) < HD
-
-    @pl.when(polar)
-    def _():
-        @pl.loop(1, lon_n)
-        def _(o):
-            cap_copy(o).wait_recv()
-
-        kv = jnp.concatenate([cap_recv[t, :STRIP] for t in range(lon_n)], axis=0)
-        key_group = jnp.concatenate(
-            [cap_recv[t, STRIP + HD :].astype(f32)[:1] for t in range(lon_n)], axis=1
-        )
-        diagonal = lax.broadcasted_iota(jnp.int32, (STRIP, STRIP), 0) == lax.broadcasted_iota(
-            jnp.int32, (STRIP, STRIP), 1
-        )
-
-        def block(s):
-            packed = cap_recv[s, STRIP : STRIP + HD].astype(f32)
-            q = jnp.concatenate([packed, swap_halves(packed)], axis=0)
-            q = jnp.where(left, q, 0.0).astype(bf16)
-            ids = cap_recv[s, STRIP + HD :].astype(f32)[:1]
-            group = jnp.sum(jnp.where(diagonal, ids, 0.0), axis=1, keepdims=True)
-            scores = jnp.where(group == key_group, dot_t(q, kv), masked_score)
-            result = dot(softmax_bf16(scores), kv)
-            return jnp.where(left, swap_halves(result[:HD]), result[HD:]).astype(bf16)
-
-        @pl.loop(1, HEADS)
-        def _(j):
-            ret_send[j] = block(base + lax.rem(head0 + j, HEADS))
-            ret_copy(j).start()
-
-        ret_recv[head0] = block(lon)
-
     keep = [jnp.where(left, 1.0, 0.0).astype(bf16), jnp.where(left, 0.0, 1.0).astype(bf16)]
     for a in range(2):
+        spans, scores, values = [], [], []
         for w in range(5):
             if w == 0:
                 first, count, skip = 0, QUAD, QUAD
@@ -321,10 +332,10 @@
             else:
                 first, count, skip = QUAD + 32 * (w - 1), 32, 0
             first += a * STRIP
+            rows = slice(32 * w, 32 * w + 32)
             for pair in range(PAIRS):
                 lanes = slice(pair * 128, (pair + 1) * 128)
                 v_lanes = slice(HW + pair * 128, HW + (pair + 1) * 128)
-                rows = slice(32 * w, 32 * w + 32)
                 k = jnp.concatenate([kv_ref[2 * a, rows, lanes], kv_ref[2 * a + 1, rows, lanes]], axis=0)
                 v = jnp.concatenate(
                     [kv_ref[2 * a, rows, v_lanes], kv_ref[2 * a + 1, rows, v_lanes]], axis=0
@@ -338,16 +349,26 @@
                     ],
                     axis=0,
                 )
-                result = dot(softmax_bf16(dot_t(q, k) + bias), v)
-                acc[first : first + count, lanes] = jnp.where(left, result[:count], result[count:])
+                spans.append((first, count, lanes))
+                scores.append(dot_t(q, k) + bias)
+                values.append(v)
+        scores = jnp.concatenate(scores, axis=0)
+        raised = jnp.exp(scores - jnp.max(scores, axis=-1, keepdims=True))
+        inverse = 1.0 / jnp.sum(raised, axis=-1, keepdims=True)
+        raised = raised.astype(bf16)
+        at = 0
+        for (first, count, lanes), v in zip(spans, values):
+            result = dot(raised[at : at + 2 * count], v) * inverse[at : at + 2 * count]
+            acc[first : first + count, lanes] = jnp.where(left, result[:count], result[count:])
+            at += 2 * count
 
     def add_cap(strip):
         for pair in range(PAIRS):
             lanes = slice(pair * 128, (pair + 1) * 128)
             even, odd = ret_recv[2 * pair].astype(f32), ret_recv[2 * pair + 1].astype(f32)
-            at = strip * STRIP
-            acc[at : at + HD, lanes] += jnp.where(left, even, swap_halves(odd))
-            acc[at + HD : at + STRIP, lanes] += jnp.where(left, swap_halves(even), odd)
+            at = pl.multiple_of(strip * STRIP, STRIP)
+            acc[pl.ds(at, HD), lanes] += jnp.where(left, even, swap_halves(odd))
+            acc[pl.ds(at + HD, HD), lanes] += jnp.where(left, swap_halves(even), odd)
 
     @pl.when(polar)
     def _():
@@ -355,13 +376,7 @@
         def _(j):
             ret_copy(j).wait_recv()
 
-    @pl.when(lat == 0)
-    def _():
-        add_cap(0)
-
-    @pl.when(lat == lat_n - 1)
-    def _():
-        add_cap(1)
+        add_cap(cap_strip)
 
     mixed = acc[...].astype(bf16)
     out_ref[...] = dot(one_hot(2 * STRIP, 2 * STRIP, block_token), mixed).astype(bf16)
@@ -395,15 +410,20 @@
     rows, columns, width = tokens.shape
     count = rows * columns
     vmem = pl.BlockSpec(memory_space=pltpu.VMEM)
-    anywhere = pl.BlockSpec(memory_space=pl.ANY)
+    hbm = pl.BlockSpec(memory_space=pltpu.HBM)
+    groups = cap_group.transpose(0, 2, 3, 1)
     out = pl.pallas_call(
         functools.partial(kernel, lat_n, lon_n),
         out_shape=jax.ShapeDtypeStruct((count, HW), bf16),
-        in_specs=[anywhere, vmem, anywhere, vmem, vmem, vmem],
+        in_specs=[hbm] * 6,
         out_specs=vmem,
         scratch_shapes=[
             pltpu.VMEM((count, width), bf16),
             pltpu.VMEM(w_qkv.shape, bf16),
+            pltpu.VMEM((1, width), f32),
+            pltpu.VMEM(bias_table.shape, f32),
+            pltpu.VMEM(bias_index.shape, jnp.int32),
+            pltpu.VMEM(groups.shape, jnp.int32),
             pltpu.VMEM((count, width), bf16),
             pltpu.VMEM((2 * EXT + 4 * QUAD, width), bf16),
             pltpu.VMEM((count, HW), bf16),
@@ -414,7 +434,7 @@
             pltpu.VMEM((HEADS, HD, 128), bf16),
             pltpu.VMEM((HEADS, HD, 128), bf16),
             pltpu.VMEM((count, HW), f32),
-            pltpu.SemaphoreType.DMA((2,)),
+            pltpu.SemaphoreType.DMA((6,)),
             pltpu.SemaphoreType.DMA((10,)),
             pltpu.SemaphoreType.DMA((10,)),
             pltpu.SemaphoreType.DMA((lon_n,)),
@@ -423,11 +443,11 @@
             pltpu.SemaphoreType.DMA((HEADS,)),
         ],
         compiler_params=pltpu.CompilerParams(
-            collective_id=0, has_side_effects=True, vmem_limit_bytes=48 * 1024 * 1024
+            collective_id=0, has_side_effects=True, vmem_limit_bytes=63 * 1024 * 1024
         ),
     )(
         tokens.reshape(count, width), ln_gain.reshape(1, width), w_qkv, bias_table, bias_index,
-        cap_group.reshape(cap_group.shape[:3]),
+        groups,
     )
     return out.reshape(rows, columns, HW)
 

time: 45.2 us -> 27.8 us (0.62)
  the two profiles are of different devices: /device:TPU:7 before, /device:TPU:1 now
where the time goes in v2:
time: 27.8 us; the launch traced here: 27.7 us
  Pallas kernels  26 us (94%)
  local copies, waits for them, and re-layouts  1.67 us (6%)
    pallas_call x1, Pallas kernels, local(): pl.pallas_call(functools.partial(kernel, lat_n, lon_n), out_shape=jax.Sha...  26 us
    unnamed x1, local copies, waits for them, and re-layouts  1.67 us

profile of v2, /device:TPU:1, one launch (start us, length us, event | category | flops | bytes accessed | tf_op | source)
XLA Modules:
  0.0 27.7 jit_solution(4409392256966207618)
XLA Ops:
  0.0 26.0 %shard_map.64 = bf16[256,512]{1,0:T(8,128)(2,1)} custom-call(bf16[256,1024]{1,0:T(8,128)(2,1)} %bitcast.5, f32[1,1024]{1,0:T(1,128)} %bitcast.6, bf16[1024,1536]{1,0:T(8,128)(2,1)} %w_hbm.1, f32[8,225]{1,0:T(8,128)} %table_hbm.1, s32[64,64]{1,0:T(8,128)} %index_hbm.1, s32[2,4,1,8]{3,2,1,0:T(1,128)} %bitcast.7), custom_call_target="tpu_custom_call" | custom-call | tf_op jit(solution)/shard_map/pallas_call | solution.py:415
  26.0 1.7 %copy.8 = bf16[8,32,512]{2,1,0:T(8,128)(2,1)} copy(bf16[8,32,512]{2,1,0:T(8,128)(2,1)} %bitcast.4) | data formatting | bytes 524288

commit v3 on v2

--- a/solution.py
+++ b/solution.py
@@ -55,11 +55,6 @@
     values = values - center
     spread = jnp.mean(values * values, axis=-1, keepdims=True)
     return (values * lax.rsqrt(spread + epsilon) * gain).astype(bf16)
-
-
-def softmax_bf16(scores):
-    raised = jnp.exp(scores - jnp.max(scores, axis=-1, keepdims=True))
-    return (raised * (1.0 / jnp.sum(raised, axis=-1, keepdims=True))).astype(bf16)
 
 
 def swap_halves(x):
@@ -144,7 +139,7 @@
         halo_copy(9, STRIP + last, 2 * EXT + QUAD, QUAD, lat, east),
     ]
 
-    @pl.when(has_n)
+    @pl.when(has_n & (lat != 1))
     def _():
         for c in north:
             c.start()
@@ -152,6 +147,11 @@
     @pl.when(has_s)
     def _():
         for c in south:
+            c.start()
+
+    @pl.when(lat == 1)
+    def _():
+        for c in north:
             c.start()
 
     for c in sides:
@@ -222,9 +222,9 @@
     def _():
         cap_pack(cap_strip)
 
-        @pl.loop(1, lon_n)
-        def _(o):
-            cap_copy(o).start()
+        @pl.loop(0, lon_n - 1)
+        def _(k):
+            cap_copy(k + 1).start()
 
         cap_recv[lon] = cap_send[head0]
 
@@ -279,11 +279,14 @@
             ids = cap_recv[s, STRIP + HD :].astype(f32)[:1]
             group = jnp.sum(jnp.where(diagonal, ids, 0.0), axis=1, keepdims=True)
             scores = jnp.where(group == key_group, dot_t(q, kv), masked_score)
-            result = dot(softmax_bf16(scores), kv)
+            raised = jnp.exp(scores - jnp.max(scores, axis=-1, keepdims=True))
+            inverse = 1.0 / jnp.sum(raised, axis=-1, keepdims=True)
+            result = dot(raised.astype(bf16), kv) * inverse
             return jnp.where(left, swap_halves(result[:HD]), result[HD:]).astype(bf16)
 
-        @pl.loop(1, HEADS)
-        def _(j):
+        @pl.loop(0, HEADS - 1)
+        def _(k):
+            j = k + 1
             ret_send[j] = block(base + lax.rem(head0 + j, HEADS))
             ret_copy(j).start()
 

time: 27.8 us -> 27.2 us (0.978)
  Pallas kernels: 26 us -> 25.3 us
    pallas_call x1, Pallas kernels: 26 us -> 25.3 us  [local(): pl.pallas_call(functools.partial(kernel, lat_n, lon_n), out_shape=jax.Sha...]
where the time goes in v3:
time: 27.2 us; the launch traced here: 27 us
  Pallas kernels  25.3 us (93%)
  local copies, waits for them, and re-layouts  1.67 us (6%)
    pallas_call x1, Pallas kernels, local(): pl.pallas_call(functools.partial(kernel, lat_n, lon_n), out_shape=jax.Sha...  25.3 us
    unnamed x1, local copies, waits for them, and re-layouts  1.67 us

profile of v3, /device:TPU:1, one launch (start us, length us, event | category | flops | bytes accessed | tf_op | source)
XLA Modules:
  0.0 27.0 jit_solution(8445881723318549652)
XLA Ops:
  0.0 25.3 %shard_map.64 = bf16[256,512]{1,0:T(8,128)(2,1)} custom-call(bf16[256,1024]{1,0:T(8,128)(2,1)} %bitcast.5, f32[1,1024]{1,0:T(1,128)} %bitcast.6, bf16[1024,1536]{1,0:T(8,128)(2,1)} %w_hbm.1, f32[8,225]{1,0:T(8,128)} %table_hbm.1, s32[64,64]{1,0:T(8,128)} %index_hbm.1, s32[2,4,1,8]{3,2,1,0:T(1,128)} %bitcast.7), custom_call_target="tpu_custom_call" | custom-call | tf_op jit(solution)/shard_map/pallas_call | solution.py:418
  25.3 1.7 %copy.8 = bf16[8,32,512]{2,1,0:T(8,128)(2,1)} copy(bf16[8,32,512]{2,1,0:T(8,128)(2,1)} %bitcast.4) | data formatting | bytes 524288
